TPU v7x, 256 devices: a whole 4x4x8 slice. The times are simulated.
256 devices in a mesh: var: 32 (over z_lo, x, core), tp: 8 (over z_hi, y).
Axes of the slice: x: 4, y: 4, z: 8 (z_hi: 2, z_lo: 4; z = z_hi * 4 + z_lo), core: 2. Of those that a mesh axis runs over, the one named last changes fastest.
Arguments:
- parent_inputs: bfloat16 [4096, 256], P('var'), may hold values from -6 to 6
- gate_parent: bfloat16 [4096, 7168], P('var', 'tp'), may hold values from -0.09375 to 0.09375
- up_parent: bfloat16 [4096, 7168], P('var', 'tp'), may hold values from -0.09375 to 0.09375
- down_parent: bfloat16 [7168, 4096], P('tp', 'var'), may hold values from -0.0625 to 0.0625
- targets: bfloat16 [256, 4096], P('var', 'tp'), may hold values from -6 to 6
- widths: int32 [32], P('var'), may hold values from 1792 to 7168, as said below
- gains: float32 [32, 7168], P('var', 'tp'), may hold values from 0.25 to 2
Outputs:
- down_grad: bfloat16 [32, 7168, 4096], P('var', 'tp')
- gain_grad: float32 [32, 7168], P('var', 'tp')
Inputs may be any that keep to these rules, and one draw needn't show every extreme that they name: `widths`: every draw has a variant of exactly 7168 and one of exactly 1792 kept hidden units.
All inputs are finite; a program needn't handle non-finite values.
Results may differ from a plain program's by a relative error of at most 0.0059.
Values may be sent and summed in bfloat16 or wider, within the bound.
No kernel may reach another device: no remote copies, remote signals or barrier semaphores. Data moves between devices by JAX's collectives and lax.ppermute only.
A program may use at most 128 MiB of HBM per device.

v0:
```python
import jax
import jax.numpy as jnp
from jax import lax
from jax.sharding import PartitionSpec as P


def local(parent_inputs, gate_parent, up_parent, down_parent, targets, widths, gains):
    contract_rows = (((0,), (0,)), ((), ()))
    rows = parent_inputs.shape[1]
    local_ff = gate_parent.shape[1]
    feats = lax.all_gather(parent_inputs, "var", axis=0, tiled=True)
    gate_piece = lax.all_gather(gate_parent, "var", axis=0, tiled=True)
    up_piece = lax.all_gather(up_parent, "var", axis=0, tiled=True)
    gate_sum = lax.dot_general(feats, gate_piece, contract_rows, preferred_element_type=jnp.float32)
    up_sum = lax.dot_general(feats, up_piece, contract_rows, preferred_element_type=jnp.float32)
    raw = jax.nn.silu(gate_sum) * up_sum
    column = lax.axis_index("tp") * local_ff + lax.broadcasted_iota(jnp.int32, (1, local_ff), 1)
    kept = (column < widths[0]).astype(jnp.float32)
    hidden = (raw * gains * kept).astype(jnp.bfloat16)
    down_whole = lax.all_gather(down_parent, "var", axis=1, tiled=True)
    partial_value = jnp.dot(hidden, down_whole, preferred_element_type=jnp.float32)
    target_part = lax.all_gather(targets, "var", axis=0, tiled=True)
    output = lax.psum(partial_value, "tp")
    target_whole = lax.all_gather(target_part, "tp", axis=1, tiled=True)
    residual = (output - target_whole.astype(jnp.float32)).astype(jnp.bfloat16)
    scale = 1.0 / rows**0.5
    grad_down = lax.dot_general(hidden, residual, contract_rows, preferred_element_type=jnp.float32)
    grad_down = (grad_down * scale).astype(jnp.bfloat16)[None]
    back = lax.dot_general(
        residual, down_whole, (((1,), (1,)), ((), ())), preferred_element_type=jnp.float32
    )
    grad_gain = kept * jnp.sum(raw * back, axis=0, keepdims=True) * scale
    return (grad_down, grad_gain)


def solution(mesh):
    return jax.shard_map(
        local,
        mesh=mesh,
        in_specs=(
            P("var", None),
            P("var", "tp"),
            P("var", "tp"),
            P("tp", "var"),
            P("var", "tp"),
            P("var"),
            P("var", "tp"),
        ),
        out_specs=(P("var", "tp", None), P("var", "tp")),
        check_vma=False,
    )
```

profile of v0, /device:TPU:1, one launch (start us, length us, event | category | flops | bytes accessed | tf_op | source)
XLA Modules:
  0.0 589.8 jit_solution(13577693330374438191)
XLA Ops:
  7.2 0.0 all-gather.6.cloned.1.call-start
  7.2 0.7 all-gather.6.cloned.1.call-update
  7.9 0.0 all-gather.8.cloned.1.call-start
  7.9 0.7 all-gather.8.cloned.1.call-update
  8.6 0.0 all-gather.10.cloned.1.call-start
  8.7 0.7 all-gather.10.cloned.1.call-update
  9.4 0.0 all-gather.12.cloned.1.call-start
  9.4 0.5 all-gather.12.cloned.1.call-update
  10.0 0.0 all-gather.14.cloned.1.call-start
  10.0 49.5 %all_gather.22 = bf16[256,512]{1,0:T(8,128)(2,1)} all-gather(bf16[8,512]{1,0:T(8,128)(2,1)} %param.11), channel_id=1, replica_groups=mesh['var'=32,'tp'=8] {'var'}, dimensions={0}, use_global_device_ids=true | all-gather | bytes 270336 | tf_op jit(solution)/shard_map/all_gather | solution.py:22
  59.5 0.0 all-reduce.2.cloned.1.call-start
  60.2 0.7 reduce
  60.9 13.4 %all-gather.6.cloned.1.call-done = bf16[4096,256]{1,0:T(8,128)(2,1)} async-done(((bf16[128,256]{1,0:T(8,128)(2,1)}), bf16[4096,256]{1,0:T(8,128)(2,1)}) %all-gather.6.cloned.1.call-update) | async-done | bytes 2097168 | tf_op jit(solution)/shard_map/all_gather | solution.py:11
  74.4 69.0 %all-gather.8.cloned.1.call-done = bf16[4096,896]{1,0:T(8,128)(2,1)} async-done(((bf16[128,896]{1,0:T(8,128)(2,1)}), bf16[4096,896]{1,0:T(8,128)(2,1)}) %all-gather.8.cloned.1.call-update) | async-done | bytes 7340048 | tf_op jit(solution)/shard_map/all_gather | solution.py:12
  143.3 7.0 %fusion.5 = f32[256,896]{1,0:T(8,128)} fusion(bf16[4096,256]{1,0:T(8,128)(2,1)} %all-gather.6.cloned.1.call-done, bf16[4096,896]{1,0:T(8,128)(2,1)} %all-gather.8.cloned.1.call-done), kind=kOutput, calls=%fused_computation.12 | convolution fusion | flops 1879048192 | bytes 10354688 | tf_op jit(solution)/shard_map/dot_general | solution.py:14
  150.3 61.7 %all-gather.10.cloned.1.call-done = bf16[4096,896]{1,0:T(8,128)(2,1)} async-done(((bf16[128,896]{1,0:T(8,128)(2,1)}), bf16[4096,896]{1,0:T(8,128)(2,1)}) %all-gather.10.cloned.1.call-update) | async-done | bytes 7340048 | tf_op jit(solution)/shard_map/all_gather | solution.py:13
  212.1 5.7 convolution_multiply_fusion.1
  217.7 77.8 %all-gather.12.cloned.1.call-done = bf16[896,4096]{1,0:T(8,128)(2,1)} async-done(((bf16[896,128]{1,0:T(8,128)(2,1)}), bf16[896,4096]{1,0:T(8,128)(2,1)}) %all-gather.12.cloned.1.call-update) | async-done | bytes 7340048 | tf_op jit(solution)/shard_map/all_gather | solution.py:20
  295.5 7.4 %fusion.2 = f32[256,4096]{1,0:T(8,128)} fusion(bf16[896,4096]{1,0:T(8,128)(2,1)} %all-gather.12.cloned.1.call-done, f32[256,896]{1,0:T(8,128)S(1)} %convolution_multiply_fusion.1, f32[896]{0:T(1024)S(1)} %fusion.3, f32[896]{0:T(1024)S(1)} %reduce), kind=kOutput, calls=%fused_computation.7 | convolution fusion | flops 1879736320 | bytes 12459008 | tf_op jit(solution)/shard_map/dot_general | solution.py:21
  303.0 68.9 %all-gather.14.cloned.1.call-done = bf16[256,4096]{1,0:T(8,128)(2,1)} async-done(((bf16[256,512]{1,0:T(8,128)(2,1)}), bf16[256,4096]{1,0:T(8,128)(2,1)}) %all-gather.14.cloned.1.call-update) | async-done | bytes 2097168 | tf_op jit(solution)/shard_map/all_gather | solution.py:24
  371.9 197.8 %all-reduce.2.cloned.1.call-done = f32[256,4096]{1,0:T(8,128)} async-done(((f32[256,4096]{1,0:T(8,128)}), f32[256,4096]{1,0:T(8,128)}) %all-reduce.2.cloned.1.call-update) | async-done | bytes 4194320 | tf_op jit(solution)/shard_map/psum | solution.py:23
  569.7 7.4 %fusion.1 = f32[896]{0:T(1024)S(1)} fusion(f32[256,896]{1,0:T(8,128)S(1)} %convolution_multiply_fusion.1, bf16[896,4096]{1,0:T(8,128)(2,1)} %all-gather.12.cloned.1.call-done, f32[256,4096]{1,0:T(8,128)} %all-reduce.2.cloned.1.call-done, bf16[256,4096]{1,0:T(8,128)(2,1)} %all-gather.14.cloned.1.call-done), kind=kOutput, calls=%fused_computation.5 | convolution fusion | flops 1882651776 | bytes 14552576 | tf_op jit(solution)/shard_map/dot_general | solution.py:29
  577.1 0.6 fusion.4
  577.7 5.2 fusion
  (9 shorter events, 0.1 us)
Async XLA Ops:
  7.2 67.2 %all-gather.6.cloned.1.call-start = ((), (), s32[]{:S(2)}) async-start(), calls=%async_computation | async-start | bytes 2162688 | tf_op jit(solution)/shard_map/all_gather | solution.py:11
  7.9 135.4 %all-gather.8.cloned.1.call-start = ((), (), s32[]{:S(2)}) async-start(), calls=%async_computation.1 | async-start | bytes 7569408 | tf_op jit(solution)/shard_map/all_gather | solution.py:12
  8.6 203.4 %all-gather.10.cloned.1.call-start = ((), (), s32[]{:S(2)}) async-start(), calls=%async_computation.2 | async-start | bytes 7569408 | tf_op jit(solution)/shard_map/all_gather | solution.py:13
  9.4 286.1 %all-gather.12.cloned.1.call-start = ((), (), s32[]{:S(2)}) async-start(), calls=%async_computation.3 | async-start | bytes 7569408 | tf_op jit(solution)/shard_map/all_gather | solution.py:20
  10.0 361.9 %all-gather.14.cloned.1.call-start = ((), (), s32[]{:S(2)}) async-start(), calls=%async_computation.5 | async-start | bytes 2359296 | tf_op jit(solution)/shard_map/all_gather | solution.py:24
  59.5 510.2 %all-reduce.2.cloned.1.call-start = ((), (), s32[]{:S(2)}) async-start(), calls=%async_computation.4 | async-start | bytes 8388608 | tf_op jit(solution)/shard_map/psum | solution.py:23
  74.4 137.7 %copy-start = (bf16[4096,256]{1,0:T(8,128)(2,1)S(1)}, bf16[4096,256]{1,0:T(8,128)(2,1)}, u32[]{:S(2)}) copy-start(bf16[4096,256]{1,0:T(8,128)(2,1)} %all-gather.6.cloned.1.call-done) | copy-start | bytes 6291460
  371.9 205.8 %copy-start.2 = (bf16[256,4096]{1,0:T(8,128)(2,1)S(1)}, bf16[256,4096]{1,0:T(8,128)(2,1)}, u32[]{:S(2)}) copy-start(bf16[256,4096]{1,0:T(8,128)(2,1)} %all-gather.14.cloned.1.call-done) | copy-start | bytes 6291460
  569.7 8.1 %copy-start.1 = (f32[256,4096]{1,0:T(8,128)S(1)}, f32[256,4096]{1,0:T(8,128)}, u32[]{:S(2)}) copy-start(f32[256,4096]{1,0:T(8,128)} %all-reduce.2.cloned.1.call-done) | copy-start | bytes 12582916
Sparse Core Ops, SparseCore 0:
  9.9 64.4 all-gather.5
  76.2 67.0 all-gather.7
  145.2 66.8 all-gather.9
  213.7 81.7 all-gather.11
  297.8 74.0 all-gather.13
  375.0 194.6 all-reduce.1
where the time goes:
time: 590 us
  waiting for transfers between devices  491 us (83%)
  blocking collectives  49.5 us (8%)
  matrix products  32.8 us (6%)
  between operations  14.8 us (3%)
    psum x1, waiting for transfers between devices, local(): output = lax.psum(partial_value, 'tp')  198 us
    all_gather x1, waiting for transfers between devices, local(): down_whole = lax.all_gather(down_parent, 'var', axis=1, tiled=True)  77.8 us
    all_gather x1, waiting for transfers between devices, local(): gate_piece = lax.all_gather(gate_parent, 'var', axis=0, tiled=True)  69 us
    all_gather x1, waiting for transfers between devices, local(): target_whole = lax.all_gather(target_part, 'tp', axis=1, tiled=True)  68.9 us
    all_gather x1, waiting for transfers between devices, local(): up_piece = lax.all_gather(up_parent, 'var', axis=0, tiled=True)  61.7 us
    all_gather x1, blocking collectives, local(): target_part = lax.all_gather(targets, 'var', axis=0, tiled=True)  49.5 us
    all_gather x1, waiting for transfers between devices, local(): feats = lax.all_gather(parent_inputs, 'var', axis=0, tiled=True)  13.4 us
  transfers between devices with their start and end apart: 6, of which 6 were waited for; matrix products, arithmetic and copies ran while one was open for 4% of the time, Pallas kernels for 0%

commit v1 on v0

--- a/solution.py
+++ b/solution.py
@@ -8,7 +8,9 @@
     contract_rows = (((0,), (0,)), ((), ()))
     rows = parent_inputs.shape[1]
     local_ff = gate_parent.shape[1]
-    feats = lax.all_gather(parent_inputs, "var", axis=0, tiled=True)
+    feats = jnp.concatenate(
+        lax.all_to_all(jnp.stack([parent_inputs] * lax.axis_size("var")), "var", 0, 0), axis=0
+    )
     gate_piece = lax.all_gather(gate_parent, "var", axis=0, tiled=True)
     up_piece = lax.all_gather(up_parent, "var", axis=0, tiled=True)
     gate_sum = lax.dot_general(feats, gate_piece, contract_rows, preferred_element_type=jnp.float32)

time: 590 us -> 562 us (0.953)
  waiting for transfers between devices: 491 us -> 411 us
  blocking collectives: 49.5 us -> 90.4 us
  starting transfers between devices: 0.23 us -> 10.2 us
    all_gather x1, waiting for transfers between devices: 69 us -> 1.92 us  [local(): gate_piece = lax.all_gather(gate_parent, 'var', axis=0, tiled=True)]
    all_gather x1, blocking collectives: 49.5 us -> 90.4 us  [local(): target_part = lax.all_gather(targets, 'var', axis=0, tiled=True)]
    all_gather x1 -> x0, waiting for transfers between devices: 13.4 us -> none  [local(): feats = lax.all_gather(parent_inputs, 'var', axis=0, tiled=True)]
    all_to_all x0 -> x1, starting transfers between devices: none -> 10 us  [local(): lax.all_to_all(jnp.stack([parent_inputs] * lax.axis_size('var')), 'var',...]
  transfers between devices with their start and end apart: 6 -> 6, of which waited for: 6 -> 5; matrix products, arithmetic and copies ran while one was open for 4% -> 4% of each run, Pallas kernels for 0% -> 0%
where the time goes in v1:
time: 562 us
  waiting for transfers between devices  411 us (73%)
  blocking collectives  90.4 us (16%)
  matrix products  32.1 us (6%)
  between operations  14.5 us (3%)
  starting transfers between devices  10.2 us (2%)
    psum x1, waiting for transfers between devices, local(): output = lax.psum(partial_value, 'tp')  198 us
    all_gather x1, blocking collectives, local(): target_part = lax.all_gather(targets, 'var', axis=0, tiled=True)  90.4 us
    all_gather x1, waiting for transfers between devices, local(): down_whole = lax.all_gather(down_parent, 'var', axis=1, tiled=True)  77.9 us
    all_gather x1, waiting for transfers between devices, local(): target_whole = lax.all_gather(target_part, 'tp', axis=1, tiled=True)  68.9 us
    all_gather x1, waiting for transfers between devices, local(): up_piece = lax.all_gather(up_parent, 'var', axis=0, tiled=True)  62.8 us
  transfers between devices with their start and end apart: 6, of which 5 were waited for; matrix products, arithmetic and copies ran while one was open for 4% of the time, Pallas kernels for 0%

profile of v1, /device:TPU:1, one launch (start us, length us, event | category | flops | bytes accessed | tf_op | source)
XLA Modules:
  0.0 561.7 jit_solution(8641350675801830565)
XLA Ops:
  7.2 0.0 all-gather.5.cloned.1.call-start
  7.2 0.7 all-gather.5.cloned.1.call-update
  7.9 0.0 all-gather.7.cloned.1.call-start
  8.0 0.7 all-gather.7.cloned.1.call-update
  8.7 0.0 all-gather.9.cloned.1.call-start
  8.7 0.7 all-gather.9.cloned.1.call-update
  9.4 2.4 stack.2
  11.8 10.0 %all-to-all-start = ((bf16[32,128,256]{2,1,0:T(8,128)(2,1)}), bf16[32,128,256]{2,1,0:T(8,128)(2,1)S(1)}, u32[]{:S(2)}, u32[]{:S(2)}) async-start(bf16[32,128,256]{2,1,0:T(8,128)(2,1)} %stack.2), calls=%async_computation | async-start | bytes 4194304 | tf_op jit(solution)/shard_map/all_to_all | solution.py:12
  21.8 0.0 all-gather.11.cloned.1.call-start
  21.9 90.4 %all_gather.18 = bf16[256,512]{1,0:T(8,128)(2,1)} all-gather(bf16[8,512]{1,0:T(8,128)(2,1)S(1)} %copy-done.2), channel_id=1, replica_groups=mesh['var'=32,'tp'=8] {'var'}, dimensions={0}, use_global_device_ids=true | all-gather | bytes 270336 | tf_op jit(solution)/shard_map/all_gather | solution.py:24
  112.3 0.0 all-gather.11.cloned.1.call-update
  112.3 0.0 all-reduce.2.cloned.1.call-start
  113.0 1.9 all-gather.5.cloned.1.call-done
  115.0 6.4 %fusion.5 = f32[256,896]{1,0:T(8,128)} fusion(bf16[4096,256]{1,0:T(8,128)(2,1)S(1)} %bitcast.12, bf16[4096,896]{1,0:T(8,128)(2,1)} %all-gather.5.cloned.1.call-done), kind=kOutput, calls=%fused_computation.12 | convolution fusion | flops 1879048192 | bytes 10354688 | tf_op jit(solution)/shard_map/dot_general | solution.py:16
  121.3 62.8 %all-gather.7.cloned.1.call-done = bf16[4096,896]{1,0:T(8,128)(2,1)} async-done(((bf16[128,896]{1,0:T(8,128)(2,1)}), bf16[4096,896]{1,0:T(8,128)(2,1)}) %all-gather.7.cloned.1.call-update) | async-done | bytes 7340048 | tf_op jit(solution)/shard_map/all_gather | solution.py:15
  184.1 5.7 %convolution_multiply_fusion.1 = f32[256,896]{1,0:T(8,128)S(1)} fusion(bf16[4096,256]{1,0:T(8,128)(2,1)S(1)} %bitcast.13, bf16[4096,896]{1,0:T(8,128)(2,1)} %all-gather.7.cloned.1.call-done, f32[256,896]{1,0:T(8,128)} %fusion.5), kind=kOutput, calls=%fused_computation.4 | convolution fusion | flops 1880195072 | bytes 11272192 | tf_op jit(solution)/shard_map/dot_general | solution.py:17
  189.8 77.9 %all-gather.9.cloned.1.call-done = bf16[896,4096]{1,0:T(8,128)(2,1)} async-done(((bf16[896,128]{1,0:T(8,128)(2,1)}), bf16[896,4096]{1,0:T(8,128)(2,1)}) %all-gather.9.cloned.1.call-update) | async-done | bytes 7340048 | tf_op jit(solution)/shard_map/all_gather | solution.py:22
  267.7 7.4 %fusion.2 = f32[256,4096]{1,0:T(8,128)} fusion(bf16[896,4096]{1,0:T(8,128)(2,1)} %all-gather.9.cloned.1.call-done, f32[256,896]{1,0:T(8,128)S(1)} %convolution_multiply_fusion.1, f32[896]{0:T(1024)S(1)} %fusion.3, f32[896]{0:T(1024)S(1)} %reduce), kind=kOutput, calls=%fused_computation.7 | convolution fusion | flops 1879736320 | bytes 12459008 | tf_op jit(solution)/shard_map/dot_general | solution.py:23
  275.2 0.0 all-reduce.2.cloned.1.call-update
  275.2 68.9 %all-gather.11.cloned.1.call-done = bf16[256,4096]{1,0:T(8,128)(2,1)} async-done(((bf16[256,512]{1,0:T(8,128)(2,1)}), bf16[256,4096]{1,0:T(8,128)(2,1)}) %all-gather.11.cloned.1.call-update) | async-done | bytes 2097168 | tf_op jit(solution)/shard_map/all_gather | solution.py:26
  344.1 197.7 %all-reduce.2.cloned.1.call-done = f32[256,4096]{1,0:T(8,128)} async-done(((f32[256,4096]{1,0:T(8,128)}), f32[256,4096]{1,0:T(8,128)}) %all-reduce.2.cloned.1.call-update) | async-done | bytes 4194320 | tf_op jit(solution)/shard_map/psum | solution.py:25
  541.9 7.4 %fusion.1 = f32[896]{0:T(1024)S(1)} fusion(f32[256,896]{1,0:T(8,128)S(1)} %convolution_multiply_fusion.1, bf16[896,4096]{1,0:T(8,128)(2,1)} %all-gather.9.cloned.1.call-done, f32[256,4096]{1,0:T(8,128)} %all-reduce.2.cloned.1.call-done, bf16[256,4096]{1,0:T(8,128)(2,1)} %all-gather.11.cloned.1.call-done), kind=kOutput, calls=%fused_computation.5 | convolution fusion | flops 1882651776 | bytes 14552576 | tf_op jit(solution)/shard_map/dot_general | solution.py:31
  549.3 0.6 fusion.4
  549.9 5.2 fusion
  (11 shorter events, 0.0 us)
Async XLA Ops:
  7.2 14.7 %copy-start.2 = (bf16[8,512]{1,0:T(8,128)(2,1)S(1)}, bf16[8,512]{1,0:T(8,128)(2,1)}, u32[]{:S(2)}) copy-start(bf16[8,512]{1,0:T(8,128)(2,1)} %param.11) | copy-start | bytes 24580
  7.2 105.8 %copy-start.3 = (f32[1,896]{1,0:T(1,128)S(1)}, f32[1,896]{1,0:T(1,128)}, u32[]{:S(2)}) copy-start(f32[1,896]{1,0:T(1,128)} %param.13) | copy-start | bytes 10756
  7.2 107.8 %all-gather.5.cloned.1.call-start = ((), (), s32[]{:S(2)}) async-start(), calls=%async_computation.1 | async-start | bytes 7569408 | tf_op jit(solution)/shard_map/all_gather | solution.py:14
  7.9 176.2 %all-gather.7.cloned.1.call-start = ((), (), s32[]{:S(2)}) async-start(), calls=%async_computation.2 | async-start | bytes 7569408 | tf_op jit(solution)/shard_map/all_gather | solution.py:15
  8.7 259.0 %all-gather.9.cloned.1.call-start = ((), (), s32[]{:S(2)}) async-start(), calls=%async_computation.3 | async-start | bytes 7569408 | tf_op jit(solution)/shard_map/all_gather | solution.py:22
  11.8 101.2 %all-to-all-start = ((bf16[32,128,256]{2,1,0:T(8,128)(2,1)}), bf16[32,128,256]{2,1,0:T(8,128)(2,1)S(1)}, u32[]{:S(2)}, u32[]{:S(2)}) async-start(bf16[32,128,256]{2,1,0:T(8,128)(2,1)} %stack.2), calls=%async_computation | async-start | bytes 4194304 | tf_op jit(solution)/shard_map/all_to_all | solution.py:12
  21.8 322.3 %all-gather.11.cloned.1.call-start = ((), (), s32[]{:S(2)}) async-start(), calls=%async_computation.5 | async-start | bytes 2359296 | tf_op jit(solution)/shard_map/all_gather | solution.py:26
  112.3 429.6 %all-reduce.2.cloned.1.call-start = ((), (), s32[]{:S(2)}) async-start(), calls=%async_computation.4 | async-start | bytes 8388608 | tf_op jit(solution)/shard_map/psum | solution.py:25
  344.1 205.8 %copy-start.1 = (bf16[256,4096]{1,0:T(8,128)(2,1)S(1)}, bf16[256,4096]{1,0:T(8,128)(2,1)}, u32[]{:S(2)}) copy-start(bf16[256,4096]{1,0:T(8,128)(2,1)} %all-gather.11.cloned.1.call-done) | copy-start | bytes 6291460
  541.9 8.0 %copy-start = (f32[256,4096]{1,0:T(8,128)S(1)}, f32[256,4096]{1,0:T(8,128)}, u32[]{:S(2)}) copy-start(f32[256,4096]{1,0:T(8,128)} %all-reduce.2.cloned.1.call-done) | copy-start | bytes 12582916
Sparse Core Ops, SparseCore 0:
  9.9 105.0 all-gather.4
  116.8 67.2 all-gather.6
  185.9 81.7 all-gather.8
  270.0 74.0 all-gather.10
  347.2 194.6 all-reduce.1
